TPU v7x, 128 devices: a whole 4x4x4 slice. The times are simulated.
128 devices in a mesh: dp: 16 (over z_lo, x, core), seq: 8 (over y, z_hi).
Axes of the slice: x: 4, y: 4, z: 4 (z_hi: 2, z_lo: 2; z = z_hi * 2 + z_lo), core: 2. Of those that a mesh axis runs over, the one named last changes fastest.
Arguments:
- hidden_in: bfloat16 [16, 1024, 2048], P('dp', 'seq'), may hold values from -6 to 6
- norm1_gain: bfloat16 [2048], P(('dp', 'seq')), may hold values from 0.099609375 to 1.8984375
- query_weight: bfloat16 [2048, 256], P(('dp', 'seq')), may hold values from -0.125 to 0.125
- key_weight: bfloat16 [2048, 256], P(('dp', 'seq')), may hold values from -0.125 to 0.125
- value_weight: bfloat16 [2048, 2048], P(('dp', 'seq')), may hold values from -0.125 to 0.125
- out_weight: bfloat16 [2048, 2048], P(('dp', 'seq')), may hold values from -1 to 1
- norm2_gain: bfloat16 [2048], P(('dp', 'seq')), may hold values from 0.099609375 to 1.8984375
- gate_weight: bfloat16 [2048, 5504], P(('dp', 'seq')), may hold values from -0.125 to 0.125
- up_weight: bfloat16 [2048, 5504], P(('dp', 'seq')), may hold values from -0.125 to 0.125
- down_weight: bfloat16 [2048, 5504], P(('dp', 'seq')), may hold values from -0.078125 to 0.078125
- cotangent: bfloat16 [16, 1024, 2048], P('dp', 'seq'), may hold values from -6 to 6
- source_id: int32 [16], P('dp'), may hold values from 0 to 7
- source_counts: int32 [8], replicated, may hold values from 1 to 64
Outputs:
- layer_out: bfloat16 [16, 1024, 2048], P('dp', 'seq')
- grad_in: float32 [16, 1024, 2048], P('dp', 'seq')
- grad_norm1: float32 [2048], P(('dp', 'seq'))
- grad_query: float32 [2048, 256], P(('dp', 'seq'))
- grad_key: float32 [2048, 256], P(('dp', 'seq'))
- grad_value: float32 [2048, 2048], P(('dp', 'seq'))
- grad_out: float32 [2048, 2048], P(('dp', 'seq'))
- grad_norm2: float32 [2048], P(('dp', 'seq'))
- grad_gate: float32 [2048, 5504], P(('dp', 'seq'))
- grad_up: float32 [2048, 5504], P(('dp', 'seq'))
- grad_down: float32 [2048, 5504], P(('dp', 'seq'))
All inputs are finite; a program needn't handle non-finite values.
Results may differ from a plain program's by a relative error of at most 0.025.
Values may be sent and summed in bfloat16 or wider, within the bound.
A program may use at most 192 MiB of HBM per device.

v0:
```python
import jax
import jax.numpy as jnp
import numpy as np
from jax import lax
from jax.experimental import pallas as pl
from jax.experimental.pallas import tpu as pltpu
from jax.sharding import Mesh, PartitionSpec as P

FEAT = 16
HEAD_V = 128
PAD_FF = 768
ATT_W = 640
QK_AT = slice(512, 640)
OUT_AT = slice(256, 512)
VALUE_AT = slice(0, 256)
EARLY_W = 2 * PAD_FF + 256
LATE_W = 384

norm_eps = 1e-05
AXES = ("zlo", "x", "core", "y", "zhi")
DP = ("zlo", "x", "core")
SEQ = ("y", "zhi")

MESH = pl.DeviceIdType.MESH
VMEM_LIMIT = 61 * 2**20
PIECES = 4
TILE = 256
STEP = 16
BF16, F32 = jnp.bfloat16, jnp.float32


def row_scale(source_id, source_counts):
    picked = jnp.sum(
        jnp.where(
            source_id[:, None] == jnp.arange(source_counts.shape[0], dtype=jnp.int32)[None, :],
            source_counts[None, :],
            0,
        ),
        axis=1,
    )
    return 4.0 / jnp.sqrt(picked.astype(F32))


def lane_order(back):
    at = np.arange(256)
    to = (at // 16 % 2) * 128 + (at // 32) * 16 + at % 16
    hot = np.zeros((256, 256), np.float32)
    hot[at, to] = 1.0
    return jnp.asarray(hot.T if back else hot, BF16)


def place():
    z = lax.axis_index("zhi") * 2 + lax.axis_index("zlo")
    return lax.axis_index("x"), lax.axis_index("y"), z, lax.axis_index("core")


def around(index):
    return lax.rem(index + 8, 4)


def at_y(y):
    return {"y": around(y)}


def at_core(core):
    return {"core": core}


def at_xz(x, z):
    x, z = around(x), around(z)
    return {"x": x, "zhi": z // 2, "zlo": lax.rem(z, 2)}


def ring_peers(y, core):
    return [at_y(y + 1), at_y(y - 1), at_core(1 - core)]


def plane_peers(x, z):
    return [at_xz(x + 1, z), at_xz(x - 1, z), at_xz(x, z + 1), at_xz(x, z - 1)]


def group_peers(y, core):
    return [
        (lax.rem(core + dc, 2), lax.rem(y + dy, 4))
        for dc in (0, 1)
        for dy in range(4)
        if (dc, dy) != (0, 0)
    ]


def hello(devices, partner=None, swaps=None):
    barrier = pltpu.get_barrier_semaphore()
    for device in devices:
        pl.semaphore_signal(barrier, inc=1, device_id=device, device_id_type=MESH)
    count = len(devices)
    if partner is not None:

        @pl.when(swaps)
        def _():
            pl.semaphore_signal(barrier, inc=1, device_id=partner, device_id_type=MESH)

        count = count + jnp.where(swaps, 1, 0)

    def wait():
        pl.semaphore_wait(barrier, count)

    return wait


class Copies:
    def __init__(self, send, recv):
        self.send, self.recv, self.used, self.open = send, recv, 0, []

    def start(self, src, dst, device):
        copy = pltpu.make_async_remote_copy(
            src_ref=src,
            dst_ref=dst,
            send_sem=self.send.at[self.used],
            recv_sem=self.recv.at[self.used],
            device_id=device,
            device_id_type=MESH,
        )
        copy.start()
        self.used += 1
        self.open.append(copy)
        return copy

    def local(self, src, dst):
        copy = pltpu.make_async_copy(src, dst, self.send.at[self.used])
        copy.start()
        self.used += 1
        return copy

    def swap(self, src, dst, partner, swaps):
        at = self.used
        self.used += 1

        def over():
            return pltpu.make_async_remote_copy(
                src_ref=src,
                dst_ref=dst,
                send_sem=self.send.at[at],
                recv_sem=self.recv.at[at],
                device_id=partner,
                device_id_type=MESH,
            )

        def stay():
            return pltpu.make_async_copy(src, dst, self.send.at[at])

        @pl.when(swaps)
        def _():
            over().start()

        @pl.when(jnp.logical_not(swaps))
        def _():
            stay().start()

        def wait():
            @pl.when(swaps)
            def _():
                over().wait()

            @pl.when(jnp.logical_not(swaps))
            def _():
                stay().wait()

        return wait

    def finish(self):
        for copy in self.open:
            copy.wait_send()


def way(piece):
    return 1 if piece % 2 == 0 else -1


def slab(ref, block, rows, piece=None):
    if piece is None:
        return ref.at[pl.ds(pl.multiple_of(block * rows, 128), rows)]
    size = rows // PIECES
    return ref.at[pl.ds(pl.multiple_of(block * rows + piece * size, 32), size)]


def row_steps(start, size, act, step=STEP):
    @pl.loop(0, size // step, unroll=min(4, size // step))
    def _(at):
        act(pl.ds(pl.multiple_of(start + at * step, step), step))


class GatherRing:
    def __init__(self, copies, to, mine, full, block_of, me, rows):
        self.copies, self.to, self.full, self.block_of = copies, to, full, block_of
        self.me, self.rows, self.sent, self.onward = me, rows, {}, {}
        size = rows // PIECES
        for piece in range(PIECES):
            for step in (way(piece), -way(piece)):
                self.sent[step, piece] = copies.start(
                    mine.at[pl.ds(piece * size, size)],
                    slab(full, block_of(me), rows, piece),
                    to(me + step),
                )

    def forward(self):
        for piece in range(PIECES):
            step = way(piece)
            self.sent[step, piece].wait_recv()
            here = slab(self.full, self.block_of(self.me - step), self.rows, piece)
            self.onward[piece] = self.copies.start(here, here, self.to(self.me + step))

    def near(self):
        for piece in range(PIECES):
            self.sent[-way(piece), piece].wait_recv()

    def far(self):
        for piece in range(PIECES):
            self.onward[piece].wait_recv()


class GatherTokens:
    def __init__(self, copies, mine, full, y, core):
        self.copies, self.full, self.y, self.core = copies, full, y, core
        self.rows = mine.shape[0]
        self.shared = {}
        self.own = copies.local(mine, slab(full, self.block_of(y), self.rows))
        self.shared[0] = copies.start(mine, slab(full, self.block_of(y), self.rows), at_core(1 - core))
        self.ring = GatherRing(copies, at_y, mine, full, self.block_of, y, self.rows)

    def block_of(self, index):
        return around(index) * 2 + self.core

    def share(self, k):
        here = slab(self.full, self.block_of(self.y + k), self.rows)
        self.shared[k] = self.copies.start(here, here, at_core(1 - self.core))

    def forward(self):
        self.ring.forward()

    def near(self):
        self.ring.near()
        self.share(1)
        self.share(-1)

    def far(self):
        self.ring.far()
        self.share(2)

    def finish(self):
        self.own.wait()
        for copy in self.shared.values():
            copy.wait_recv()


class GatherPlane:
    def __init__(self, copies, mine, full, x, z, core):
        self.copies, self.full = copies, full
        rows = mine.shape[0]

        def block(a, b):
            a, b = around(a), around(b)
            return jnp.where(core == 0, 4 * b + a, 4 * a + b)

        first, second = jnp.where(core == 0, x, z), jnp.where(core == 0, z, x)

        def to_first(index):
            return at_xz(jnp.where(core == 0, index, x), jnp.where(core == 0, z, index))

        def to_second(index):
            return at_xz(jnp.where(core == 0, x, index), jnp.where(core == 0, index, z))

        def onto(k, source=None):
            a = first + k
            if source is None:
                source = slab(full, block(a, second), rows)
            return GatherRing(copies, to_second, source, full, lambda b: block(a, b), second, rows)

        self.onto = onto
        self.own = copies.local(mine, slab(full, block(first, second), rows))
        self.ring = GatherRing(
            copies, to_first, mine, full, lambda a: block(a, second), first, rows
        )
        self.rings = {0: onto(0, mine)}

    def stages(self):
        def one():
            self.ring.forward()

        def two():
            self.ring.near()
            self.rings[1] = self.onto(1)
            self.rings[-1] = self.onto(-1)

        def three():
            self.rings[0].forward()

        def four():
            self.ring.far()
            self.rings[2] = self.onto(2)

        def five():
            self.rings[1].forward()
            self.rings[-1].forward()

        def six():
            self.rings[2].forward()
            self.rings[0].near()
            self.rings[0].far()

        def seven():
            for k in (1, -1, 2):
                self.rings[k].near()
                self.rings[k].far()
            self.own.wait()

        return [one, two, three, four, five, six, seven]


class ReduceRing:
    def __init__(self, copies, to, me, read, out, got, rows, source=None):
        self.copies, self.to, self.me, self.read = copies, to, me, read
        self.out, self.got, self.rows, self.source, self.sent = out, got, rows, source, {}
        self.size = rows // PIECES

    def span(self, piece):
        return pl.ds(piece * self.size, self.size)

    def push(self, slot, k, piece, device):
        span = self.span(piece)
        if self.source is not None:
            ref = self.source(k, span)
        else:

            def fill(rows):
                self.out[slot, rows] = self.read(k, rows).astype(BF16)

            row_steps(piece * self.size, self.size, fill)
            ref = self.out.at[slot, span]
        self.sent[slot, piece] = self.copies.start(ref, self.got.at[slot, span], device)

    def far(self, pieces=range(PIECES)):
        for piece in pieces:
            self.push(0, 2, piece, self.to(self.me + way(piece)))

    def direct(self, k):
        for piece in range(PIECES):
            if way(piece) == -k:
                self.push(1, k, piece, self.to(self.me + k))

    def onward(self, k):
        slot = 2 if self.source is None else 0
        for piece in range(PIECES):
            if way(piece) == k:
                self.sent[0, piece].wait_recv()

                def fill(rows):
                    self.out[slot, rows] = (
                        self.read(k, rows) + self.got[0, rows].astype(F32)
                    ).astype(BF16)

                row_steps(piece * self.size, self.size, fill)
                span = self.span(piece)
                self.sent[2, piece] = self.copies.start(
                    self.out.at[slot, span], self.got.at[2, span], self.to(self.me + k)
                )

    def arrive(self, piece):
        self.sent[1, piece].wait_recv()
        self.sent[2, piece].wait_recv()

    def total(self, rows):
        return self.read(0, rows) + self.got[1, rows].astype(F32) + self.got[2, rows].astype(F32)


class ReduceTokens:
    def __init__(self, copies, make, y, core, own, sib, got_sib, out, got):
        self.copies, self.make, self.y, self.core = copies, make, y, core
        self.own, self.sib, self.got_sib, self.shared = own, sib, got_sib, {}
        self.ring = ReduceRing(copies, at_y, y, self.read, out, got, own.shape[1])

    def read(self, k, rows):
        return self.own[k % 4, rows] + self.got_sib[k % 4, rows].astype(F32)

    def share(self, k):
        self.shared[k] = self.copies.start(
            self.sib.at[k % 4], self.got_sib.at[k % 4], at_core(1 - self.core)
        )

    def part(self, k):
        self.make(k, self.own.at[k % 4], self.sib.at[k % 4])
        self.share(k)

    def one(self):
        self.shared[2].wait_recv()
        self.ring.far()
        self.shared[1].wait_recv()
        self.ring.direct(1)

    def two(self):
        self.shared[-1].wait_recv()
        self.ring.direct(-1)
        self.ring.onward(1)
        self.ring.onward(-1)
        self.shared[0].wait_recv()

    def each(self, act):
        for piece in range(PIECES):
            self.ring.arrive(piece)

            def take(rows):
                act(rows, self.ring.total(rows))

            row_steps(piece * self.ring.size, self.ring.size, take)


class ReducePlane:
    def __init__(self, copies, parts, lanes, x, z, core, out1, got1, mid, out2, got2, sent=None):
        rows = mid.shape[1]
        sent = parts if sent is None else sent

        def block(a, b):
            a, b = around(a), around(b)
            return jnp.where(core == 0, 4 * b + a, 4 * a + b)

        last, first = jnp.where(core == 0, x, z), jnp.where(core == 0, z, x)

        def to_last(index):
            return at_xz(jnp.where(core == 0, index, x), jnp.where(core == 0, z, index))

        def to_first(index):
            return at_xz(jnp.where(core == 0, x, index), jnp.where(core == 0, index, z))

        def ring(k):
            def place_of(step, span):
                start = block(last + k, first + step) * rows + span.start
                return pl.ds(pl.multiple_of(start, STEP), span.size)

            def read(step, span):
                return parts[place_of(step, span), lanes].astype(F32)

            def source(step, span):
                return sent.at[place_of(step, span), lanes]

            return ReduceRing(copies, to_first, first, read, out1.at[k % 4], got1.at[k % 4], rows, source)

        self.mid = mid
        self.rings = {k: ring(k) for k in (2, 1, -1, 0)}

        def read2(step, span):
            return mid[step % 4, span].astype(F32)

        def source2(step, span):
            return mid.at[step % 4, span]

        self.ring = ReduceRing(copies, to_last, last, read2, out2, got2, rows, source2)

    def start(self):
        for ring in self.rings.values():
            ring.far()

    def direct(self):
        for ring in self.rings.values():
            ring.direct(1)
            ring.direct(-1)

    def onward(self, k):
        self.rings[k].onward(1)
        self.rings[k].onward(-1)

    def middle(self, k):
        ring = self.rings[k]
        for piece in range(PIECES):
            ring.arrive(piece)

            def fill(rows):
                self.mid[k % 4, rows] = ring.total(rows).astype(BF16)

            row_steps(piece * ring.size, ring.size, fill)

    def stages(self):
        def ends(k, then):
            def act():
                self.middle(k)
                then()

            return act

        return (
            [self.start, self.direct]
            + [lambda k=k: self.onward(k) for k in (2, 1, -1, 0)]
            + [
                ends(2, self.ring.far),
                ends(1, lambda: self.ring.direct(1)),
                ends(-1, lambda: self.ring.direct(-1)),
                ends(0, lambda: None),
                lambda: (self.ring.onward(1), self.ring.onward(-1)),
            ]
        )

    def each(self, act):
        for piece in range(PIECES):
            self.ring.arrive(piece)

            def take(rows):
                act(rows, self.ring.total(rows))

            row_steps(piece * self.ring.size, self.ring.size, take)


def nt(left, right):
    return lax.dot_general(left, right, (((1,), (1,)), ((), ())), preferred_element_type=F32)


def tn(left, right):
    return lax.dot_general(left, right, (((0,), (0,)), ((), ())), preferred_element_type=F32)


def nn(left, right):
    return jnp.dot(left, right, preferred_element_type=F32)


def chip_rows(block):
    return pl.ds(pl.multiple_of(block * 256, 256), 256)


def part_maker(pairs, y, core):
    def make(k, mine, theirs):
        rows = chip_rows(around(y + k))

        @pl.loop(0, mine.shape[-1] // TILE)
        def _(tile):
            columns = pl.ds(pl.multiple_of(tile * TILE, TILE), TILE)
            total = None
            for left, right, lanes in pairs:
                term = nt(left[rows, :], right[columns, lanes])
                total = term if total is None else total + term
            low, high = total[:128], total[128:]
            mine[:, columns] = jnp.where(core == 0, low, high)
            theirs[:, columns] = jnp.where(core == 0, high, low).astype(BF16)

    return make


def inverse_of(value):
    return lax.rsqrt(jnp.mean(value * value, axis=-1, keepdims=True) + norm_eps)


def norm_back_rows(grad, value, gain):
    inverse = inverse_of(value)
    unit = value * inverse
    scaled = grad * gain
    moved = inverse * (scaled - unit * jnp.mean(scaled * unit, axis=-1, keepdims=True))
    return moved, grad * unit


def reorder_into(target, source, hot):
    runs = source.shape[1] // 256
    for run in range(runs):
        moved = nn(source[:, run * 256 : (run + 1) * 256], hot[...]).astype(BF16)
        target[:, run * 128 : (run + 1) * 128] = moved[:, :128]
        target[:, (runs + run) * 128 : (runs + run + 1) * 128] = moved[:, 128:]


def gain_rows(att):
    row = lax.broadcasted_iota(jnp.int32, (8, 128), 0)
    lane = lax.broadcasted_iota(jnp.int32, (8, 128), 1)
    pick = jnp.where((lane == row + 64) & (row < 2), 1.0, 0.0).astype(BF16)
    return nt(pick, att[:, QK_AT])


def head_lanes(head):
    lane = lax.broadcasted_iota(jnp.int32, (1, 128), 1)
    return (lane >= head * FEAT) & (lane < (head + 1) * FEAT)


def scores_of(q, k, block, extent):
    x = nt(q, k) * 0.25
    row = lax.broadcasted_iota(jnp.int32, (256, extent), 0) + block * 256
    keep = row >= lax.broadcasted_iota(jnp.int32, (256, extent), 1)
    return x, jnp.where(keep, 1.0 + x + 0.5 * (x * x), 0.0), keep


def forward_kernel(
    hidden,
    cotangent,
    scale,
    hot,
    query,
    key,
    value,
    out_weight,
    gate,
    up,
    down,
    gain_pair,
    att_out,
    weights,
    raw_out,
    low_out,
    qs,
    ks,
    values,
    attended,
    shares,
    inverses,
    gains,
    raw,
    top,
    middle,
    normed2,
    att_cut,
    mlp_cut,
    raw_cut,
    top_cut,
    att_own,
    mlp_own,
    raw_all,
    att_all,
    att_scaled,
    own,
    sib,
    got_sib,
    out,
    got,
    low,
    send,
    recv,
):
    x, y, z, core = place()
    zhi = z // 2
    partner = {"core": 1 - core, "zhi": 1 - zhi}
    swaps = core != zhi
    peers = group_peers(y, core)
    ready = hello(
        [{"core": c, "y": d} for c, d in peers] + plane_peers(x, z), partner, swaps
    )
    copies = Copies(send, recv)
    me = core * 4 + y
    depth, here = gate.shape[0], gate.shape[1] // 8

    def spread(cuts, target):
        rows = pl.ds(pl.multiple_of(me * depth, depth), depth)
        kept = copies.local(cuts.at[me], target.at[rows])
        got = [
            copies.start(cuts.at[c * 4 + d], target.at[rows], {"core": c, "y": d}) for c, d in peers
        ]

        def wait():
            kept.wait()
            for copy in got:
                copy.wait_recv()

        return wait

    reorder_into(raw_cut, hidden, hot)
    gap = jnp.zeros((depth, 62), BF16)
    for block in range(8):
        att_cut[block, :, VALUE_AT] = value[:, block * 256 : (block + 1) * 256]
        att_cut[block, :, OUT_AT] = out_weight[:, block * 256 : (block + 1) * 256]
        att_cut[block, :, QK_AT] = jnp.concatenate(
            (
                query[:, block * 32 : (block + 1) * 32],
                key[:, block * 32 : (block + 1) * 32],
                gain_pair[...],
                gap,
            ),
            axis=1,
        )
    ready()
    wait_raw = copies.swap(raw_cut, raw, partner, swaps)
    wait_att = spread(att_cut, att_own)
    gap = jnp.zeros((depth, PAD_FF - here), BF16)
    for block in range(8):
        for at, weight in enumerate((gate, up, down)):
            cut = weight[:, block * here : (block + 1) * here]
            mlp_cut[block, :, at * PAD_FF : (at + 1) * PAD_FF] = jnp.concatenate((cut, gap), axis=1)
    wait_raw()
    tokens = GatherTokens(copies, raw, raw_all, y, core)
    wait_mlp = spread(mlp_cut, mlp_own)

    def weigh(rows):
        top_cut[rows] = (cotangent[rows].astype(F32) * scale[...]).astype(BF16)

    row_steps(0, top_cut.shape[0], weigh)
    reorder_into(top_cut, top_cut[...], hot)
    wait_att()
    plane = GatherPlane(copies, att_own, att_all, x, z, core)
    wait_top = copies.swap(top_cut, top, partner, swaps)

    def invert(block):
        def act(rows):
            inverse = inverse_of(raw_all[rows].astype(F32))
            inverses[rows] = jnp.broadcast_to(inverse, (STEP, 128))

        row_steps(block * 128, 128, act)

    one, two, three, four, five, six, seven = plane.stages()
    one()
    two()
    tokens.forward()
    three()
    four()
    tokens.shared[0].wait_recv()
    tokens.own.wait()
    invert(2 * y)
    invert(2 * y + 1)
    five()
    six()
    wait_mlp()
    mlp_plane = GatherPlane(copies, mlp_own, weights, x, z, core)
    mlp_stages = iter(mlp_plane.stages())
    tokens.near()
    invert(2 * around(y + 1) + core)
    invert(2 * around(y - 1) + core)
    tokens.far()
    invert(2 * around(y + 2) + core)
    seven()
    gains[...] = gain_rows(att_all)

    def scale_rows(rows):
        gain = att_all[rows, 576:577].astype(F32)
        att_scaled[rows, 0:256] = (att_all[rows, VALUE_AT].astype(F32) * gain).astype(BF16)
        att_scaled[rows, 256:384] = (att_all[rows, QK_AT].astype(F32) * gain).astype(BF16)

    row_steps(0, att_all.shape[0], scale_rows, 128)
    tokens.shared[1].wait_recv()
    tokens.shared[-1].wait_recv()
    invert(2 * around(y + 1) + 1 - core)
    invert(2 * around(y - 1) + 1 - core)
    tokens.shared[2].wait_recv()
    invert(2 * around(y + 2) + 1 - core)
    wait_top()
    tops = GatherTokens(copies, top, low_out, y, core)
    kept = [copies.local(att_all, att_out), copies.local(raw_all, raw_out)]

    @pl.loop(0, 2, unroll=True)
    def _(half):
        rows = pl.ds(pl.multiple_of(half * 512, 512), 512)
        inverse = inverses[rows]
        block = raw_all[rows]
        both = nn(block, att_scaled[:, 0:256])
        values[rows] = (both * jnp.concatenate((inverse, inverse), axis=1)).astype(BF16)
        both = nn(block, att_scaled[:, 256:384]) * inverse
        lane = lax.broadcasted_iota(jnp.int32, (1, 128), 1)
        qs[rows] = jnp.where(lane < 32, both, 0.0).astype(BF16)
        ks[rows] = jnp.where(lane < 32, pltpu.roll(both, 96, 1), 0.0).astype(BF16)

    for head in range(2):
        lanes = slice(head * HEAD_V, (head + 1) * HEAD_V)
        for block in range(4):
            rows, extent = slice(block * 256, (block + 1) * 256), (block + 1) * 256
            q = jnp.where(head_lanes(head), qs[rows], 0)
            unused, scores, unused_keep = scores_of(q, ks[0:extent], block, extent)
            share = 1.0 / jnp.sum(scores, axis=-1, keepdims=True)
            numer = nn(scores.astype(BF16), values[0:extent, lanes])
            attended[rows, lanes] = (numer * share).astype(BF16)
            shares[rows, lanes] = jnp.broadcast_to(share, (256, HEAD_V))
    for _ in range(3):
        next(mlp_stages)()
    tops.forward()
    sums = ReduceTokens(
        copies, part_maker([(attended, att_all, OUT_AT)], y, core), y, core, own, sib, got_sib, out, got
    )
    for k in (2, 1, -1):
        sums.part(k)
    sums.one()
    sums.part(0)
    next(mlp_stages)()
    sums.two()
    next(mlp_stages)()
    tops.near()

    def norm2(rows, total):
        value = raw[rows].astype(F32) + total
        middle[rows] = value
        low[rows] = (value * inverse_of(value) * gains[1:2]).astype(BF16)

    sums.each(norm2)
    back = GatherTokens(copies, low, normed2, y, core)
    next(mlp_stages)()
    tops.far()
    back.forward()
    back.near()
    back.far()
    next(mlp_stages)()
    tops.finish()
    back.finish()
    for copy in kept:
        copy.wait()
    copies.finish()


def mlp_kernel(
    normed2_in,
    low_in,
    weights_in,
    middle,
    top,
    gains,
    grad_middle,
    grad_gain,
    middle_low,
    grads,
    gate_sum,
    layer_parts,
    normed2,
    grad_low,
    weights,
    hidden,
    gate_act,
    up_act,
    own,
    sib,
    got_sib,
    out,
    got,
    sib2,
    got_sib2,
    layer,
    low,
    plane_out1,
    plane_got1,
    plane_mid,
    plane_out2,
    plane_got2,
    send,
    recv,
):
    x, y, z, core = place()
    copies = Copies(send, recv)
    ready = hello(ring_peers(y, core) + plane_peers(x, z))
    order = (2, 1, -1, 0)
    loads = {}

    def load(k):
        slot = order.index(k)
        for at, owner in enumerate((core, 1 - core)):
            block = around(y + k) * 2 + owner
            rows = pl.ds(slot * 256 + at * 128, 128)
            for source, target in ((normed2_in, normed2), (low_in, grad_low)):
                loads.setdefault(k, []).append(copies.local(slab(source, block, 128), target.at[rows]))

    def lanes(at):
        return slice(at * PAD_FF, (at + 1) * PAD_FF)

    load(2)
    load(1)
    loads["w"] = [copies.local(weights_in.at[:, lanes(at)], weights.at[:, lanes(at)]) for at in range(3)]
    load(-1)
    load(0)
    ready()

    def act_tile(half, tile):
        rows = slice(half * 512, (half + 1) * 512)
        here = slice(tile * TILE, (tile + 1) * TILE)

        def cut(at):
            return weights[:, at * PAD_FF + tile * TILE : at * PAD_FF + (tile + 1) * TILE]

        block = normed2[rows]
        gate = nn(block, cut(0))
        upward = nn(block, cut(1))
        grad_hidden = nn(grad_low[rows], cut(2))
        sigma = jax.nn.sigmoid(gate)
        silu = gate * sigma
        hidden[rows, here] = (silu * upward).astype(BF16)
        slope = sigma + silu * (1.0 - sigma)
        gate_act[rows, here] = (grad_hidden * upward * slope).astype(BF16)
        up_act[rows, here] = (grad_hidden * silu).astype(BF16)

    def part_pair(half, pairs, sib_ref):
        rows = slice(half * 512, (half + 1) * 512)

        @pl.loop(0, own.shape[-1] // 512)
        def _(tile):
            columns = pl.ds(pl.multiple_of(tile * 512, 512), 512)
            total = None
            for left, right in pairs:
                term = nt(left[rows, :], weights[columns, right])
                total = term if total is None else total + term
            for at in range(2):
                k = order[2 * half + at] % 4
                own[k, :, columns] = total[at * 256 : at * 256 + 128]
                sib_ref[k, :, columns] = total[at * 256 + 128 : at * 256 + 256].astype(BF16)

    def grad_block(at, left, right):
        @pl.loop(0, left.shape[1] // 512)
        def _(tile):
            columns = pl.ds(pl.multiple_of(tile * 512, 512), 512)
            weights[columns, lanes(at)] = tn(left[:, columns], right[...]).astype(BF16)

    sums = ReduceTokens(copies, None, y, core, own, sib, got_sib, out, got)
    acts = [(gate_act, lanes(0)), (up_act, lanes(1))]
    for copy in loads[2] + loads[1] + loads["w"]:
        copy.wait()
    for tile in range(3):
        act_tile(0, tile)
    part_pair(0, acts, sib)
    sums.share(2)
    sums.share(1)
    for copy in loads[-1] + loads[0]:
        copy.wait()
    act_tile(1, 0)
    sums.one()
    act_tile(1, 1)
    act_tile(1, 2)
    part_pair(1, acts, sib)
    sums.share(-1)
    sums.share(0)
    sums.two()
    grad_block(0, normed2, gate_act)
    plane = ReducePlane(
        copies, weights, lanes(0), x, z, core, plane_out1, plane_got1, plane_mid, plane_out2, plane_got2
    )
    stages = iter(plane.stages())
    next(stages)()
    grad_gain[...] = jnp.zeros_like(grad_gain)

    def back(rows, total):
        moved, terms = norm_back_rows(total, middle[rows], gains[1:2])
        grad_gain[...] += terms[:8] + terms[8:]
        value = top[rows].astype(F32) + moved
        grad_middle[rows] = value
        low[rows] = value.astype(BF16)

    sums.each(back)
    gather = GatherTokens(copies, low, middle_low, y, core)
    next(stages)()
    grad_block(1, normed2, up_act)
    layers = ReduceTokens(copies, None, y, core, own, sib2, got_sib2, None, None)
    part_pair(0, [(hidden, lanes(2))], sib2)
    layers.share(2)
    layers.share(1)
    gather.forward()
    for _ in range(4):
        next(stages)()
    part_pair(1, [(hidden, lanes(2))], sib2)
    layers.share(-1)
    layers.share(0)
    gather.near()
    grad_block(2, grad_low, hidden)
    stored = [
        copies.local(weights.at[:, PAD_FF : 3 * PAD_FF], grads),
    ]
    for _ in range(4):
        next(stages)()
    gather.far()
    for stage in stages:
        stage()
    for k in order:
        layers.shared[k].wait_recv()

        def add(rows, k=k):
            layer[k % 4, rows] = layers.read(k, rows).astype(BF16)

        row_steps(0, 128, add)
    stored.append(copies.local(layer, layer_parts))

    def take(rows, total):
        gate_sum[rows] = total.astype(BF16)

    plane.each(take)
    gather.finish()
    for copy in stored:
        copy.wait()
    copies.finish()


def back_kernel(
    low_in,
    raw_in,
    att,
    qs,
    ks,
    values,
    attended,
    shares,
    inverses,
    raw,
    grad_middle,
    middle,
    gains,
    grad_gain2,
    grads_in,
    layer_in,
    gate_sum,
    late_out,
    early_out,
    gate_out,
    grad_in,
    layer_out,
    gain_out,
    tokens,
    early,
    late,
    layer_parts,
    grad_numer,
    grad_denom,
    grad_q,
    grad_k,
    grad_v,
    grad_qk,
    grad_values,
    scaled_qk,
    scaled_values,
    own,
    sib,
    got_sib,
    out,
    got,
    layer_sent,
    layer_got,
    early_out1,
    early_got1,
    early_mid,
    early_out2,
    early_got2,
    late_out1,
    late_got1,
    late_mid,
    late_out2,
    late_got2,
    early_sum,
    late_sum,
    last,
    layer,
    gain_part,
    gain_got,
    gain_sum,
    gain_back,
    send,
    recv,
):
    x, y, z, core = place()
    zhi = z // 2
    partner = {"core": 1 - core, "zhi": 1 - zhi}
    swaps = core != zhi
    copies = Copies(send, recv)
    peers = group_peers(y, core)
    planes = [
        (lax.rem(x + dx, 4), lax.rem(z + dz, 4))
        for dx in range(4)
        for dz in range(4)
        if (dx, dz) != (0, 0)
    ]
    ready = hello(
        [{"core": c, "y": d} for c, d in peers] + [at_xz(a, b) for a, b in planes], partner, swaps
    )
    load_low = copies.local(low_in, tokens)
    load_early = copies.local(grads_in, early.at[:, 0 : 2 * PAD_FF])
    load_layer = copies.local(layer_in, layer_parts)
    ready()
    layers = ReduceRing(
        copies,
        at_y,
        y,
        lambda k, rows: layer_parts[k % 4, rows].astype(F32),
        layer_sent,
        layer_got,
        128,
        lambda k, span: layer_in.at[k % 4, span],
    )
    layers.far()
    layers.direct(1)
    layers.direct(-1)
    load_low.wait()

    @pl.loop(0, tokens.shape[1] // 512)
    def _(tile):
        columns = pl.ds(pl.multiple_of(tile * 512, 512), 512)
        early[columns, 2 * PAD_FF : EARLY_W] = tn(tokens[:, columns], attended[...]).astype(BF16)

    load_early.wait()
    early_plane = ReducePlane(
        copies,
        early,
        slice(0, EARLY_W),
        x,
        z,
        core,
        early_out1,
        early_got1,
        early_mid,
        early_out2,
        early_got2,
    )
    early_stages = iter(early_plane.stages())
    next(early_stages)()
    me = core * 4 + y
    back_copies, local = [], []

    def send_back(sums_ref, out_ref):
        def cut(index):
            return sums_ref.at[pl.ds(pl.multiple_of(index * 16, 16), 16)]

        local.append(copies.local(cut(me), out_ref.at[me]))
        for c, d in peers:
            back_copies.append(copies.start(cut(c * 4 + d), out_ref.at[me], {"core": c, "y": d}))

    send_back(gate_sum, gate_out)

    @pl.loop(0, 2, unroll=True)
    def _(half):
        rows = pl.ds(pl.multiple_of(half * 512, 512), 512)
        grad_mixed = nn(tokens[rows], att[:, OUT_AT]).astype(BF16).astype(F32)
        numer = grad_mixed * shares[rows]
        grad_numer[rows] = numer.astype(BF16)
        product = numer * attended[rows].astype(F32)
        for head in range(2):
            lanes = slice(head * HEAD_V, (head + 1) * HEAD_V)
            total = -jnp.sum(product[:, lanes], axis=-1, keepdims=True)
            grad_denom[rows, lanes] = jnp.broadcast_to(total, (512, HEAD_V))

    load_raw = copies.local(raw_in, tokens)
    grad_k[...] = jnp.zeros_like(grad_k)
    grad_v[...] = jnp.zeros_like(grad_v)

    def attend_back(head, block):
        lanes = slice(head * HEAD_V, (head + 1) * HEAD_V)
        rows, extent = slice(block * 256, (block + 1) * 256), (block + 1) * 256
        q = jnp.where(head_lanes(head), qs[rows], 0)
        k = ks[0:extent]
        half, scores, keep = scores_of(q, k, block, extent)
        numer = grad_numer[rows, lanes]
        total = grad_denom[rows, head * HEAD_V : head * HEAD_V + 1]
        grad_scores = nt(numer, values[0:extent, lanes]) + total
        grad_s = jnp.where(keep, grad_scores * (0.25 + 0.25 * half), 0.0).astype(BF16)
        moved = nn(grad_s, k)
        if head == 0:
            grad_q[rows] = jnp.where(head_lanes(0), moved, 0.0)
        else:
            grad_q[rows] += jnp.where(head_lanes(1), moved, 0.0)
        grad_k[0:extent] += tn(grad_s, q)
        grad_v[0:extent, lanes] += tn(scores.astype(BF16), numer)

    for block in range(4):
        attend_back(0, block)
    next(early_stages)()
    for block in range(4):
        attend_back(1, block)

    def join(rows):
        inverse = inverses[rows]
        both = grad_q[rows] + pltpu.roll(grad_k[rows], 32, 1)
        grad_qk[rows] = both.astype(BF16)
        scaled_qk[rows] = (both * inverse).astype(BF16)
        both = grad_v[rows]
        grad_values[rows] = both.astype(BF16)
        scaled_values[rows] = (both * jnp.concatenate((inverse, inverse), axis=1)).astype(BF16)

    row_steps(0, 1024, join, 128)
    sums = ReduceTokens(
        copies,
        part_maker([(grad_values, att, VALUE_AT), (grad_qk, att, QK_AT)], y, core),
        y,
        core,
        own,
        sib,
        got_sib,
        out,
        got,
    )
    sums.part(2)
    sums.part(1)
    for _ in range(4):
        next(early_stages)()
    sums.one()
    sums.part(-1)
    sums.part(0)
    load_layer.wait()
    layers.onward(1)
    layers.onward(-1)
    load_raw.wait()

    @pl.loop(0, tokens.shape[1] // 512)
    def _(tile):
        columns = pl.ds(pl.multiple_of(tile * 512, 512), 512)
        left = tokens[:, columns]
        gain = att[columns, 576:577].astype(F32)
        late[columns, 0:256] = (tn(left, scaled_values[...]) * gain).astype(BF16)
        late[columns, 256:LATE_W] = (tn(left, scaled_qk[...]) * gain).astype(BF16)

    late_plane = ReducePlane(
        copies,
        late,
        slice(0, LATE_W),
        x,
        z,
        core,
        late_out1,
        late_got1,
        late_mid,
        late_out2,
        late_got2,
    )
    late_stages = iter(late_plane.stages())
    next(late_stages)()
    sums.two()
    next(late_stages)()
    for _ in range(4):
        next(late_stages)()

    def take(target):
        def act(rows, total):
            target[rows] = total.astype(BF16)

        return act

    gain_part[...] = jnp.zeros_like(gain_part)

    def back(rows, total):
        moved, terms = norm_back_rows(total, raw[rows].astype(F32), gains[0:1])
        gain_part[...] += terms[:8] + terms[8:]
        last[rows] = (grad_middle[rows] + moved).astype(BF16)

    sums.each(back)
    waits = [copies.swap(last, grad_in, partner, swaps)]
    row = lax.broadcasted_iota(jnp.int32, (8, 1), 0)
    gain_part[...] = jnp.where(
        row == 0,
        jnp.sum(gain_part[...], axis=0, keepdims=True),
        jnp.where(row == 1, jnp.sum(grad_gain2[...], axis=0, keepdims=True), 0.0),
    )
    here = 4 * z + x

    def lanes_of(block):
        return pl.ds(pl.multiple_of(block * 128, 128), 128)

    gain_copies = [
        copies.start(gain_part.at[:, lanes_of(4 * b + a)], gain_got.at[here], at_xz(a, b))
        for a, b in planes
    ]
    gain_own = copies.local(gain_part.at[:, lanes_of(here)], gain_got.at[here])
    for stage in early_stages:
        stage()
    for _ in range(4):
        next(late_stages)()
    for piece in range(PIECES):
        layers.arrive(piece)

    def add(rows):
        layer[rows] = (middle[rows] + layers.total(rows)).astype(BF16)

    row_steps(0, 128, add)
    waits.append(copies.swap(layer, layer_out, partner, swaps))
    early_plane.each(take(early_sum))
    send_back(early_sum, early_out)
    for stage in late_stages:
        stage()
    for copy in gain_copies:
        copy.wait_recv()
    gain_own.wait()
    gain_sum[...] = jnp.sum(gain_got[...], axis=0)
    for c, d in peers:
        back_copies.append(copies.start(gain_sum, gain_back.at[me], {"core": c, "y": d}))
    local.append(copies.local(gain_sum, gain_back.at[me]))
    late_plane.each(take(late_sum))
    send_back(late_sum, late_out)
    for copy in back_copies:
        copy.wait_recv()
    for copy in local:
        copy.wait()
    gain_out[...] = jnp.sum(gain_back[...], axis=0)
    for wait in waits:
        wait()
    copies.finish()


def unpack_kernel(
    late, early, gates, layer, last, hot, query, key, value, out, gate, up, down, layer_out, grad_in
):
    here = gate.shape[1] // 8
    for block in range(8):
        for source, at, grad in ((gates, 0, gate), (early, 0, up), (early, 1, down)):
            cut = source[block, :, at * PAD_FF : at * PAD_FF + here]
            grad[:, block * here : (block + 1) * here] = cut.astype(F32)
        value[:, block * 256 : (block + 1) * 256] = late[block, :, 0:256].astype(F32)
        out[:, block * 256 : (block + 1) * 256] = early[block, :, 2 * PAD_FF : EARLY_W].astype(F32)
        query[:, block * 32 : (block + 1) * 32] = late[block, :, 256:288].astype(F32)
        key[:, block * 32 : (block + 1) * 32] = late[block, :, 288:320].astype(F32)
    runs = layer.shape[1] // 256
    for run in range(runs):
        for source, target in ((layer, layer_out), (last, grad_in)):
            low = source[:, run * 128 : (run + 1) * 128]
            high = source[:, (runs + run) * 128 : (runs + run + 1) * 128]
            both = jnp.concatenate((low, high), axis=1)
            target[:, run * 256 : (run + 1) * 256] = nn(both, hot[...]).astype(target.dtype)


HBM, VMEM = pl.ANY, pltpu.VMEM


def call(kernel, number, ins, outs, scratch, sems, flops):
    def spec(space):
        return pl.BlockSpec(memory_space=space)

    remote = {}
    if number is not None:
        scratch = list(scratch) + [pltpu.SemaphoreType.DMA((sems,)), pltpu.SemaphoreType.DMA((sems,))]
        remote = dict(collective_id=number, has_side_effects=True)
    return pl.pallas_call(
        kernel,
        out_shape=[jax.ShapeDtypeStruct(shape, dtype) for shape, dtype, _ in outs],
        in_specs=[spec(space) for _, space in ins],
        out_specs=[spec(space) for _, _, space in outs],
        scratch_shapes=scratch,
        compiler_params=pltpu.CompilerParams(vmem_limit_bytes=VMEM_LIMIT, **remote),
        cost_estimate=pl.CostEstimate(flops=flops, bytes_accessed=2**26, transcendentals=0),
        name=kernel.__name__,
    )(*[array for array, _ in ins])


def ring_scratch(width, own=True):
    sums = [VMEM((4, 128, width), F32)] if own else []
    return sums + [
        VMEM((4, 128, width), BF16),
        VMEM((4, 128, width), BF16),
        VMEM((3, 128, width), BF16),
        VMEM((3, 128, width), BF16),
    ]


def plane_scratch(width):
    return [
        VMEM((4, 1, 128, width), BF16),
        VMEM((4, 3, 128, width), BF16),
        VMEM((4, 128, width), BF16),
        VMEM((1, 128, width), BF16),
        VMEM((3, 128, width), BF16),
    ]


def body(
    hidden_in,
    norm1_gain,
    query_weight,
    key_weight,
    value_weight,
    out_weight,
    norm2_gain,
    gate_weight,
    up_weight,
    down_weight,
    cotangent,
    source_id,
    source_counts,
):
    rows, toks, width = hidden_in.shape
    depth, ff = gate_weight.shape
    length, held = 8 * toks, 8 * depth
    mlp_w = 3 * PAD_FF
    scale = row_scale(source_id, source_counts).reshape(1, 1)
    (
        att,
        weights,
        raw_all,
        low,
        qs,
        ks,
        values,
        attended,
        shares,
        inverses,
        gains,
        raw,
        top,
        middle,
        normed2,
    ) = call(
        forward_kernel,
        0,
        [
            (array, VMEM)
            for array in (
                hidden_in.reshape(toks, width),
                cotangent.reshape(toks, width),
                scale,
                lane_order(False),
                query_weight,
                key_weight,
                value_weight,
                out_weight,
                gate_weight,
                up_weight,
                down_weight,
                jnp.stack((norm1_gain, norm2_gain), axis=1),
            )
        ],
        [
            ((width, ATT_W), BF16, HBM),
            ((width, mlp_w), BF16, HBM),
            ((length, width), BF16, HBM),
            ((length, width), BF16, HBM),
            ((length, 128), BF16, VMEM),
            ((length, 128), BF16, VMEM),
            ((length, 256), BF16, VMEM),
            ((length, 256), BF16, VMEM),
            ((length, 256), F32, VMEM),
            ((length, 128), F32, VMEM),
            ((8, width), F32, VMEM),
            ((toks, width), BF16, VMEM),
            ((toks, width), BF16, VMEM),
            ((toks, width), F32, VMEM),
            ((length, width), BF16, HBM),
        ],
        [
            VMEM((8, depth, ATT_W), BF16),
            VMEM((8, depth, mlp_w), BF16),
            VMEM((toks, width), BF16),
            VMEM((toks, width), BF16),
            VMEM((held, ATT_W), BF16),
            VMEM((held, mlp_w), BF16),
            VMEM((length, width), BF16),
            VMEM((width, ATT_W), BF16),
            VMEM((width, 384), BF16),
        ]
        + ring_scratch(width)
        + [VMEM((toks, width), BF16)],
        240,
        4 * 10**9,
    )
    grad_middle, grad_gain2, middle_low, grads, gate_sum, layer_parts = call(
        mlp_kernel,
        1,
        [
            (normed2, HBM),
            (low, HBM),
            (weights, HBM),
            (middle, VMEM),
            (top, VMEM),
            (gains, VMEM),
        ],
        [
            ((toks, width), F32, VMEM),
            ((8, width), F32, VMEM),
            ((length, width), BF16, HBM),
            ((width, 2 * PAD_FF), BF16, HBM),
            ((held, PAD_FF), BF16, VMEM),
            ((4, toks, width), BF16, HBM),
        ],
        [
            VMEM((length, width), BF16),
            VMEM((length, width), BF16),
            VMEM((width, mlp_w), BF16),
            VMEM((length, PAD_FF), BF16),
            VMEM((length, PAD_FF), BF16),
            VMEM((length, PAD_FF), BF16),
        ]
        + ring_scratch(width)
        + [
            VMEM((4, toks, width), BF16),
            VMEM((4, toks, width), BF16),
            VMEM((4, toks, width), BF16),
            VMEM((toks, width), BF16),
        ]
        + plane_scratch(PAD_FF),
        150,
        30 * 10**9,
    )
    late_back, early_back, gate_back, last, layer, gain_sums = call(
        back_kernel,
        2,
        [
            (middle_low, HBM),
            (raw_all, HBM),
            (att, VMEM),
            (qs, VMEM),
            (ks, VMEM),
            (values, VMEM),
            (attended, VMEM),
            (shares, VMEM),
            (inverses, VMEM),
            (raw, VMEM),
            (grad_middle, VMEM),
            (middle, VMEM),
            (gains, VMEM),
            (grad_gain2, VMEM),
            (grads, HBM),
            (layer_parts, HBM),
            (gate_sum, VMEM),
        ],
        [
            ((8, depth, LATE_W), BF16, HBM),
            ((8, depth, EARLY_W), BF16, HBM),
            ((8, depth, PAD_FF), BF16, HBM),
            ((toks, width), BF16, HBM),
            ((toks, width), BF16, HBM),
            ((8, 128), F32, VMEM),
        ],
        [
            VMEM((length, width), BF16),
            VMEM((width, EARLY_W), BF16),
            VMEM((width, LATE_W), BF16),
            VMEM((4, toks, width), BF16),
            VMEM((length, 256), BF16),
            VMEM((length, 256), F32),
            VMEM((length, 128), F32),
            VMEM((length, 128), F32),
            VMEM((length, 256), F32),
            VMEM((length, 128), BF16),
            VMEM((length, 256), BF16),
            VMEM((length, 128), BF16),
            VMEM((length, 256), BF16),
        ]
        + ring_scratch(width)
        + [VMEM((1, toks, width), BF16), VMEM((3, toks, width), BF16)]
        + plane_scratch(EARLY_W)
        + plane_scratch(LATE_W)
        + [
            VMEM((held, EARLY_W), BF16),
            VMEM((held, LATE_W), BF16),
            VMEM((toks, width), BF16),
            VMEM((toks, width), BF16),
            VMEM((8, width), F32),
            VMEM((16, 8, 128), F32),
            VMEM((8, 128), F32),
            VMEM((8, 8, 128), F32),
        ],
        240,
        8 * 10**9,
    )
    grads_out = call(
        unpack_kernel,
        None,
        [(array, VMEM) for array in (late_back, early_back, gate_back, layer, last, lane_order(True))],
        [
            ((depth, query_weight.shape[1]), F32, VMEM),
            ((depth, key_weight.shape[1]), F32, VMEM),
            ((depth, value_weight.shape[1]), F32, VMEM),
            ((depth, out_weight.shape[1]), F32, VMEM),
            ((depth, ff), F32, VMEM),
            ((depth, ff), F32, VMEM),
            ((depth, ff), F32, VMEM),
            ((toks, width), BF16, VMEM),
            ((toks, width), F32, VMEM),
        ],
        [],
        0,
        0,
    )
    grad_query, grad_key, grad_value, grad_out, grad_gate, grad_up, grad_down = grads_out[:7]
    at = (lax.axis_index("core") * 4 + lax.axis_index("y")) * depth
    pair = lax.dynamic_slice(gain_sums, (0, at), (8, depth))
    return (
        grads_out[7].reshape(rows, toks, width),
        grads_out[8].reshape(rows, toks, width),
        pair[0],
        grad_query,
        grad_key,
        grad_value,
        grad_out,
        pair[1],
        grad_gate,
        grad_up,
        grad_down,
    )


def solution(mesh):
    zlo, chips_x, cores, chips_y, zhi = 2, 4, 2, 4, 2
    whole = Mesh(mesh.devices.reshape(zlo, chips_x, cores, chips_y, zhi), AXES)
    weight = P(AXES, None)
    gain = P(AXES)
    tokens = P(DP, SEQ, None)
    return jax.shard_map(
        body,
        mesh=whole,
        in_specs=(
            tokens,
            gain,
            weight,
            weight,
            weight,
            weight,
            gain,
            weight,
            weight,
            weight,
            tokens,
            P(DP),
            P(),
        ),
        out_specs=(
            tokens,
            tokens,
            gain,
            weight,
            weight,
            weight,
            weight,
            gain,
            weight,
            weight,
            weight,
        ),
        check_vma=False,
    )
```

profile of v0, /device:TPU:1, one launch (start us, length us, event | category | flops | bytes accessed | tf_op | source)
XLA Modules:
  0.0 275.7 jit_solution(12290147416524173112)
XLA Ops:
  0.6 0.7 pad_maximum_fusion
  1.3 0.7 copy.28.gain_pair
  2.7 1.3 fusion
  4.6 111.8 %forward_kernel.1 = (bf16[2048,640]{1,0:T(8,128)(2,1)}, bf16[2048,2304]{1,0:T(8,128)(2,1)}, bf16[1024,2048]{1,0:T(8,128)(2,1)}, bf16[1024,2048]{1,0:T(8,128)(2,1...) custom-call(bf16[128,2048]{1,0:T(8,128)(2,1)} %bitcast.14, ...), custom_call_target="tpu_custom_call" | custom-call | flops 4000000000 | bytes 67108864 | tf_op jit(solution)/shard_map/forward_kernel/pallas_call | solution.py:1301
  116.5 70.8 %mlp_kernel.1 = (f32[128,2048]{1,0:T(8,128)}, f32[8,2048]{1,0:T(8,128)}, bf16[1024,2048]{1,0:T(8,128)(2,1)}, bf16[2048,1536]{1,0:T(8,128)(2,1)}, bf16[128,768]{1...) custom-call(bf16[1024,2048]{1,0:T(8,128)(2,1)} %get-tuple-element.47.normed2_in, bf16[1024,2048]{1,0:T(8,128)(2,1)} %get-tuple-element.48.low_in, ...), custom_call_target="tpu_custom_call" | custom-call | flops 30000001024 | bytes 67108864 | tf_op jit(solution)/shard_map/mlp_kernel/pallas_call | solution.py:1301
  187.3 83.2 %back_kernel.1 = (bf16[8,16,384]{2,1,0:T(8,128)(2,1)}, bf16[8,16,1792]{2,1,0:T(8,128)(2,1)}, bf16[8,16,768]{2,1,0:T(8,128)(2,1)}, bf16[128,2048]{1,0:T(8,128)(2,...) custom-call(bf16[1024,2048]{1,0:T(8,128)(2,1)} %get-tuple-element.53.low_in, ...), custom_call_target="tpu_custom_call" | custom-call | flops 8000000000 | bytes 67108864 | tf_op jit(solution)/shard_map/back_kernel/pallas_call | solution.py:1301
  270.5 3.5 %unpack_kernel.1 = (f32[16,256]{1,0:T(8,128)}, f32[16,256]{1,0:T(8,128)}, f32[16,2048]{1,0:T(8,128)}, f32[16,2048]{1,0:T(8,128)}, f32[16,5504]{1,0:T(8,128)}, /*...) custom-call(bf16[8,16,384]{2,1,0:T(8,128)(2,1)} %get-tuple-element.68.late, ...), custom_call_target="tpu_custom_call" | custom-call | bytes 67108864 | tf_op jit(solution)/shard_map/unpack_kernel/pallas_call | solution.py:1301
  274.0 0.7 constant_dynamic-slice_fusion
  274.7 0.5 slice_bitcast_fusion
where the time goes:
time: 281 us; the launch traced here: 276 us
  Pallas kernels  269 us (96%)
    pallas_call x4, Pallas kernels, call(): pl.pallas_call(kernel, out_shape=[jax.ShapeDtypeStruct(shape, dtype) for...  269 us

commit v1 on v0

--- a/solution.py
+++ b/solution.py
@@ -13,7 +13,7 @@
 QK_AT = slice(512, 640)
 OUT_AT = slice(256, 512)
 VALUE_AT = slice(0, 256)
-EARLY_W = 2 * PAD_FF + 256
+EARLY_W = PAD_FF + 256
 LATE_W = 384
 
 norm_eps = 1e-05
@@ -24,6 +24,7 @@
 MESH = pl.DeviceIdType.MESH
 VMEM_LIMIT = 61 * 2**20
 PIECES = 4
+PLANE_PIECES = 2
 TILE = 256
 STEP = 16
 BF16, F32 = jnp.bfloat16, jnp.float32
@@ -176,10 +177,10 @@
     return 1 if piece % 2 == 0 else -1
 
 
-def slab(ref, block, rows, piece=None):
+def slab(ref, block, rows, piece=None, pieces=PIECES):
     if piece is None:
         return ref.at[pl.ds(pl.multiple_of(block * rows, 128), rows)]
-    size = rows // PIECES
+    size = rows // pieces
     return ref.at[pl.ds(pl.multiple_of(block * rows + piece * size, 32), size)]
 
 
@@ -190,31 +191,32 @@
 
 
 class GatherRing:
-    def __init__(self, copies, to, mine, full, block_of, me, rows):
+    def __init__(self, copies, to, mine, full, block_of, me, rows, pieces=PIECES):
         self.copies, self.to, self.full, self.block_of = copies, to, full, block_of
         self.me, self.rows, self.sent, self.onward = me, rows, {}, {}
-        size = rows // PIECES
-        for piece in range(PIECES):
+        self.pieces = pieces
+        size = rows // pieces
+        for piece in range(pieces):
             for step in (way(piece), -way(piece)):
                 self.sent[step, piece] = copies.start(
                     mine.at[pl.ds(piece * size, size)],
-                    slab(full, block_of(me), rows, piece),
+                    slab(full, block_of(me), rows, piece, pieces),
                     to(me + step),
                 )
 
     def forward(self):
-        for piece in range(PIECES):
+        for piece in range(self.pieces):
             step = way(piece)
             self.sent[step, piece].wait_recv()
-            here = slab(self.full, self.block_of(self.me - step), self.rows, piece)
+            here = slab(self.full, self.block_of(self.me - step), self.rows, piece, self.pieces)
             self.onward[piece] = self.copies.start(here, here, self.to(self.me + step))
 
     def near(self):
-        for piece in range(PIECES):
+        for piece in range(self.pieces):
             self.sent[-way(piece), piece].wait_recv()
 
     def far(self):
-        for piece in range(PIECES):
+        for piece in range(self.pieces):
             self.onward[piece].wait_recv()
 
 
@@ -273,12 +275,14 @@
             a = first + k
             if source is None:
                 source = slab(full, block(a, second), rows)
-            return GatherRing(copies, to_second, source, full, lambda b: block(a, b), second, rows)
+            return GatherRing(
+                copies, to_second, source, full, lambda b: block(a, b), second, rows, PLANE_PIECES
+            )
 
         self.onto = onto
         self.own = copies.local(mine, slab(full, block(first, second), rows))
         self.ring = GatherRing(
-            copies, to_first, mine, full, lambda a: block(a, second), first, rows
+            copies, to_first, mine, full, lambda a: block(a, second), first, rows, PLANE_PIECES
         )
         self.rings = {0: onto(0, mine)}
 
@@ -317,10 +321,11 @@
 
 
 class ReduceRing:
-    def __init__(self, copies, to, me, read, out, got, rows, source=None):
+    def __init__(self, copies, to, me, read, out, got, rows, source=None, pieces=PIECES):
         self.copies, self.to, self.me, self.read = copies, to, me, read
         self.out, self.got, self.rows, self.source, self.sent = out, got, rows, source, {}
-        self.size = rows // PIECES
+        self.pieces = pieces
+        self.size = rows // pieces
 
     def span(self, piece):
         return pl.ds(piece * self.size, self.size)
@@ -338,18 +343,18 @@
             ref = self.out.at[slot, span]
         self.sent[slot, piece] = self.copies.start(ref, self.got.at[slot, span], device)
 
-    def far(self, pieces=range(PIECES)):
-        for piece in pieces:
+    def far(self):
+        for piece in range(self.pieces):
             self.push(0, 2, piece, self.to(self.me + way(piece)))
 
     def direct(self, k):
-        for piece in range(PIECES):
+        for piece in range(self.pieces):
             if way(piece) == -k:
                 self.push(1, k, piece, self.to(self.me + k))
 
     def onward(self, k):
         slot = 2 if self.source is None else 0
-        for piece in range(PIECES):
+        for piece in range(self.pieces):
             if way(piece) == k:
                 self.sent[0, piece].wait_recv()
 
@@ -367,6 +372,15 @@
     def arrive(self, piece):
         self.sent[1, piece].wait_recv()
         self.sent[2, piece].wait_recv()
+
+    def each(self, act):
+        for piece in range(self.pieces):
+            self.arrive(piece)
+
+            def take(rows):
+                act(rows, self.total(rows))
+
+            row_steps(piece * self.size, self.size, take)
 
     def total(self, rows):
         return self.read(0, rows) + self.got[1, rows].astype(F32) + self.got[2, rows].astype(F32)
@@ -413,6 +427,22 @@
             row_steps(piece * self.ring.size, self.ring.size, take)
 
 
+def second_ring(copies, mid, x, z, core, out2, got2):
+    last = jnp.where(core == 0, x, z)
+
+    def to_last(index):
+        return at_xz(jnp.where(core == 0, index, x), jnp.where(core == 0, z, index))
+
+    def read(step, span):
+        return mid[step % 4, span].astype(F32)
+
+    def source(step, span):
+        return mid.at[step % 4, span]
+
+    rows = mid.shape[1]
+    return ReduceRing(copies, to_last, last, read, out2, got2, rows, source, PLANE_PIECES)
+
+
 class ReducePlane:
     def __init__(self, copies, parts, lanes, x, z, core, out1, got1, mid, out2, got2, sent=None):
         rows = mid.shape[1]
@@ -424,9 +454,6 @@
 
         last, first = jnp.where(core == 0, x, z), jnp.where(core == 0, z, x)
 
-        def to_last(index):
-            return at_xz(jnp.where(core == 0, index, x), jnp.where(core == 0, z, index))
-
         def to_first(index):
             return at_xz(jnp.where(core == 0, x, index), jnp.where(core == 0, index, z))
 
@@ -441,18 +468,23 @@
             def source(step, span):
                 return sent.at[place_of(step, span), lanes]
 
-            return ReduceRing(copies, to_first, first, read, out1.at[k % 4], got1.at[k % 4], rows, source)
+            return ReduceRing(
+                copies,
+                to_first,
+                first,
+                read,
+                out1.at[k % 4],
+                got1.at[k % 4],
+                rows,
+                source,
+                PLANE_PIECES,
+            )
 
         self.mid = mid
         self.rings = {k: ring(k) for k in (2, 1, -1, 0)}
 
-        def read2(step, span):
-            return mid[step % 4, span].astype(F32)
-
-        def source2(step, span):
-            return mid.at[step % 4, span]
-
-        self.ring = ReduceRing(copies, to_last, last, read2, out2, got2, rows, source2)
+        if got2 is not None:
+            self.ring = second_ring(copies, mid, x, z, core, out2, got2)
 
     def start(self):
         for ring in self.rings.values():
@@ -469,7 +501,7 @@
 
     def middle(self, k):
         ring = self.rings[k]
-        for piece in range(PIECES):
+        for piece in range(PLANE_PIECES):
             ring.arrive(piece)
 
             def fill(rows):
@@ -497,14 +529,15 @@
             ]
         )
 
+    def first_stages(self):
+        return (
+            [self.start, self.direct]
+            + [lambda k=k: self.onward(k) for k in (2, 1, -1, 0)]
+            + [lambda k=k: self.middle(k) for k in (2, 1, -1, 0)]
+        )
+
     def each(self, act):
-        for piece in range(PIECES):
-            self.ring.arrive(piece)
-
-            def take(rows):
-                act(rows, self.ring.total(rows))
-
-            row_steps(piece * self.ring.size, self.ring.size, take)
+        self.ring.each(act)
 
 
 def nt(left, right):
@@ -597,12 +630,12 @@
     weights,
     raw_out,
     low_out,
-    qs,
-    ks,
-    values,
-    attended,
-    shares,
-    inverses,
+    qs_out,
+    ks_out,
+    values_out,
+    attended_out,
+    shares_out,
+    inverses_out,
     gains,
     raw,
     top,
@@ -623,6 +656,12 @@
     out,
     got,
     low,
+    qs,
+    ks,
+    values,
+    attended,
+    shares,
+    inverses,
     send,
     recv,
 ):
@@ -713,6 +752,8 @@
     invert(2 * around(y + 1) + core)
     invert(2 * around(y - 1) + core)
     tokens.far()
+    wait_top()
+    tops = GatherTokens(copies, top, low_out, y, core)
     invert(2 * around(y + 2) + core)
     seven()
     gains[...] = gain_rows(att_all)
@@ -729,9 +770,20 @@
     invert(2 * around(y - 1) + 1 - core)
     tokens.shared[2].wait_recv()
     invert(2 * around(y + 2) + 1 - core)
-    wait_top()
-    tops = GatherTokens(copies, top, low_out, y, core)
     kept = [copies.local(att_all, att_out), copies.local(raw_all, raw_out)]
+
+    def stores():
+        pairs = (
+            (qs, qs_out),
+            (ks, ks_out),
+            (values, values_out),
+            (attended, attended_out),
+            (shares, shares_out),
+            (inverses, inverses_out),
+        )
+        for source, target in pairs:
+            kept.append(copies.local(source, target))
+
 
     @pl.loop(0, 2, unroll=True)
     def _(half):
@@ -755,9 +807,11 @@
             numer = nn(scores.astype(BF16), values[0:extent, lanes])
             attended[rows, lanes] = (numer * share).astype(BF16)
             shares[rows, lanes] = jnp.broadcast_to(share, (256, HEAD_V))
+        if head == 0:
+            tops.forward()
+    stores()
     for _ in range(3):
         next(mlp_stages)()
-    tops.forward()
     sums = ReduceTokens(
         copies, part_maker([(attended, att_all, OUT_AT)], y, core), y, core, own, sib, got_sib, out, got
     )
@@ -802,6 +856,7 @@
     middle_low,
     grads,
     gate_sum,
+    up_mid,
     layer_parts,
     normed2,
     grad_low,
@@ -823,14 +878,17 @@
     plane_mid,
     plane_out2,
     plane_got2,
+    up_out1,
+    up_got1,
     send,
     recv,
+    loads=(),
 ):
     x, y, z, core = place()
     copies = Copies(send, recv)
     ready = hello(ring_peers(y, core) + plane_peers(x, z))
     order = (2, 1, -1, 0)
-    loads = {}
+    operands, loads = loads, {}
 
     def load(k):
         slot = order.index(k)
@@ -843,12 +901,16 @@
     def lanes(at):
         return slice(at * PAD_FF, (at + 1) * PAD_FF)
 
+    def load_tile(tile):
+        cuts = [slice(at * PAD_FF + tile * TILE, at * PAD_FF + (tile + 1) * TILE) for at in range(3)]
+        loads["w", tile] = [copies.local(weights_in.at[:, cut], weights.at[:, cut]) for cut in cuts]
+
     load(2)
     load(1)
-    loads["w"] = [copies.local(weights_in.at[:, lanes(at)], weights.at[:, lanes(at)]) for at in range(3)]
-    load(-1)
-    load(0)
+    load_tile(0)
     ready()
+    for copy in operands:
+        copy.wait()
 
     def act_tile(half, tile):
         rows = slice(half * 512, (half + 1) * 512)
@@ -891,9 +953,16 @@
 
     sums = ReduceTokens(copies, None, y, core, own, sib, got_sib, out, got)
     acts = [(gate_act, lanes(0)), (up_act, lanes(1))]
-    for copy in loads[2] + loads[1] + loads["w"]:
+    for copy in loads[2] + loads[1]:
         copy.wait()
     for tile in range(3):
+        for copy in loads["w", tile]:
+            copy.wait()
+        if tile == 0:
+            load_tile(1)
+            load_tile(2)
+            load(-1)
+            load(0)
         act_tile(0, tile)
     part_pair(0, acts, sib)
     sums.share(2)
@@ -927,25 +996,33 @@
     gather = GatherTokens(copies, low, middle_low, y, core)
     next(stages)()
     grad_block(1, normed2, up_act)
+    up_plane = ReducePlane(
+        copies, weights, lanes(1), x, z, core, up_out1, up_got1, up_mid, None, None
+    )
+    up_stages = iter(up_plane.first_stages())
+    next(up_stages)()
+    for _ in range(4):
+        next(stages)()
     layers = ReduceTokens(copies, None, y, core, own, sib2, got_sib2, None, None)
     part_pair(0, [(hidden, lanes(2))], sib2)
     layers.share(2)
     layers.share(1)
     gather.forward()
-    for _ in range(4):
-        next(stages)()
+    next(up_stages)()
     part_pair(1, [(hidden, lanes(2))], sib2)
     layers.share(-1)
     layers.share(0)
+    for _ in range(4):
+        next(up_stages)()
+    for _ in range(4):
+        next(stages)()
     gather.near()
     grad_block(2, grad_low, hidden)
-    stored = [
-        copies.local(weights.at[:, PAD_FF : 3 * PAD_FF], grads),
-    ]
-    for _ in range(4):
-        next(stages)()
+    stored = [copies.local(weights.at[:, lanes(2)], grads)]
     gather.far()
     for stage in stages:
+        stage()
+    for stage in up_stages:
         stage()
     for k in order:
         layers.shared[k].wait_recv()
@@ -984,9 +1061,11 @@
     grads_in,
     layer_in,
     gate_sum,
+    up_mid,
     late_out,
     early_out,
     gate_out,
+    up_out,
     grad_in,
     layer_out,
     gain_out,
@@ -1020,6 +1099,9 @@
     late_mid,
     late_out2,
     late_got2,
+    up_out2,
+    up_got2,
+    up_sum,
     early_sum,
     late_sum,
     last,
@@ -1030,6 +1112,7 @@
     gain_back,
     send,
     recv,
+    loads=(),
 ):
     x, y, z, core = place()
     zhi = z // 2
@@ -1047,9 +1130,11 @@
         [{"core": c, "y": d} for c, d in peers] + [at_xz(a, b) for a, b in planes], partner, swaps
     )
     load_low = copies.local(low_in, tokens)
-    load_early = copies.local(grads_in, early.at[:, 0 : 2 * PAD_FF])
+    load_early = copies.local(grads_in, early.at[:, 0:PAD_FF])
     load_layer = copies.local(layer_in, layer_parts)
     ready()
+    for copy in loads:
+        copy.wait()
     layers = ReduceRing(
         copies,
         at_y,
@@ -1063,12 +1148,16 @@
     layers.far()
     layers.direct(1)
     layers.direct(-1)
+    ups = second_ring(copies, up_mid, x, z, core, up_out2, up_got2)
+    ups.far()
+    ups.direct(1)
+    ups.direct(-1)
     load_low.wait()
 
     @pl.loop(0, tokens.shape[1] // 512)
     def _(tile):
         columns = pl.ds(pl.multiple_of(tile * 512, 512), 512)
-        early[columns, 2 * PAD_FF : EARLY_W] = tn(tokens[:, columns], attended[...]).astype(BF16)
+        early[columns, PAD_FF:EARLY_W] = tn(tokens[:, columns], attended[...]).astype(BF16)
 
     load_early.wait()
     early_plane = ReducePlane(
@@ -1136,6 +1225,8 @@
     for block in range(4):
         attend_back(0, block)
     next(early_stages)()
+    ups.onward(1)
+    ups.onward(-1)
     for block in range(4):
         attend_back(1, block)
 
@@ -1195,17 +1286,18 @@
     )
     late_stages = iter(late_plane.stages())
     next(late_stages)()
+    def take(target):
+        def act(rows, total):
+            target[rows] = total.astype(BF16)
+
+        return act
+
+    ups.each(take(up_sum))
+    send_back(up_sum, up_out)
     sums.two()
     next(late_stages)()
     for _ in range(4):
         next(late_stages)()
-
-    def take(target):
-        def act(rows, total):
-            target[rows] = total.astype(BF16)
-
-        return act
-
     gain_part[...] = jnp.zeros_like(gain_part)
 
     def back(rows, total):
@@ -1267,15 +1359,15 @@
 
 
 def unpack_kernel(
-    late, early, gates, layer, last, hot, query, key, value, out, gate, up, down, layer_out, grad_in
+    late, early, gates, ups, layer, last, hot, query, key, value, out, gate, up, down, layer_out, grad_in
 ):
     here = gate.shape[1] // 8
     for block in range(8):
-        for source, at, grad in ((gates, 0, gate), (early, 0, up), (early, 1, down)):
-            cut = source[block, :, at * PAD_FF : at * PAD_FF + here]
+        for source, at, grad in ((gates, 0, gate), (ups, 0, up), (early, 0, down)):
+            cut = source[block, :, at : at + here]
             grad[:, block * here : (block + 1) * here] = cut.astype(F32)
         value[:, block * 256 : (block + 1) * 256] = late[block, :, 0:256].astype(F32)
-        out[:, block * 256 : (block + 1) * 256] = early[block, :, 2 * PAD_FF : EARLY_W].astype(F32)
+        out[:, block * 256 : (block + 1) * 256] = early[block, :, PAD_FF:EARLY_W].astype(F32)
         query[:, block * 32 : (block + 1) * 32] = late[block, :, 256:288].astype(F32)
         key[:, block * 32 : (block + 1) * 32] = late[block, :, 288:320].astype(F32)
     runs = layer.shape[1] // 256
@@ -1287,7 +1379,7 @@
             target[:, run * 256 : (run + 1) * 256] = nn(both, hot[...]).astype(target.dtype)
 
 
-HBM, VMEM = pl.ANY, pltpu.VMEM
+HBM, VMEM, LOAD = pl.ANY, pltpu.VMEM, "load"
 
 
 def call(kernel, number, ins, outs, scratch, sems, flops):
@@ -1295,6 +1387,25 @@
         return pl.BlockSpec(memory_space=space)
 
     remote = {}
+    given = kernel
+    if any(space == LOAD for _, space in ins):
+        places = [at for at, (_, space) in enumerate(ins) if space == LOAD]
+        held = [VMEM(ins[at][0].shape, ins[at][0].dtype) for at in places]
+        scratch = list(scratch) + held + [pltpu.SemaphoreType.DMA((len(held),))]
+
+        def kernel(*refs):
+            refs = list(refs)
+            send, recv = refs[-2:]
+            first = len(refs) - 3 - len(held)
+            buffers, arrived = refs[first:-3], refs[-3]
+            loads = []
+            for index, at in enumerate(places):
+                loads.append(pltpu.make_async_copy(refs[at], buffers[index], arrived.at[index]))
+                loads[-1].start()
+                refs[at] = buffers[index]
+            given(*refs[:first], send, recv, loads=loads)
+
+        ins = [(array, HBM if space == LOAD else space) for array, space in ins]
     if number is not None:
         scratch = list(scratch) + [pltpu.SemaphoreType.DMA((sems,)), pltpu.SemaphoreType.DMA((sems,))]
         remote = dict(collective_id=number, has_side_effects=True)
@@ -1306,7 +1417,7 @@
         scratch_shapes=scratch,
         compiler_params=pltpu.CompilerParams(vmem_limit_bytes=VMEM_LIMIT, **remote),
         cost_estimate=pl.CostEstimate(flops=flops, bytes_accessed=2**26, transcendentals=0),
-        name=kernel.__name__,
+        name=given.__name__,
     )(*[array for array, _ in ins])
 
 
@@ -1391,12 +1502,12 @@
             ((width, mlp_w), BF16, HBM),
             ((length, width), BF16, HBM),
             ((length, width), BF16, HBM),
-            ((length, 128), BF16, VMEM),
-            ((length, 128), BF16, VMEM),
-            ((length, 256), BF16, VMEM),
-            ((length, 256), BF16, VMEM),
-            ((length, 256), F32, VMEM),
-            ((length, 128), F32, VMEM),
+            ((length, 128), BF16, HBM),
+            ((length, 128), BF16, HBM),
+            ((length, 256), BF16, HBM),
+            ((length, 256), BF16, HBM),
+            ((length, 256), F32, HBM),
+            ((length, 128), F32, HBM),
             ((8, width), F32, VMEM),
             ((toks, width), BF16, VMEM),
             ((toks, width), BF16, VMEM),
@@ -1415,27 +1526,36 @@
             VMEM((width, 384), BF16),
         ]
         + ring_scratch(width)
-        + [VMEM((toks, width), BF16)],
-        240,
+        + [
+            VMEM((toks, width), BF16),
+            VMEM((length, 128), BF16),
+            VMEM((length, 128), BF16),
+            VMEM((length, 256), BF16),
+            VMEM((length, 256), BF16),
+            VMEM((length, 256), F32),
+            VMEM((length, 128), F32),
+        ],
+        250,
         4 * 10**9,
     )
-    grad_middle, grad_gain2, middle_low, grads, gate_sum, layer_parts = call(
+    grad_middle, grad_gain2, middle_low, grads, gate_sum, up_mid, layer_parts = call(
         mlp_kernel,
         1,
         [
             (normed2, HBM),
             (low, HBM),
             (weights, HBM),
-            (middle, VMEM),
-            (top, VMEM),
-            (gains, VMEM),
+            (middle, LOAD),
+            (top, LOAD),
+            (gains, LOAD),
         ],
         [
             ((toks, width), F32, VMEM),
             ((8, width), F32, VMEM),
             ((length, width), BF16, HBM),
-            ((width, 2 * PAD_FF), BF16, HBM),
+            ((width, PAD_FF), BF16, HBM),
             ((held, PAD_FF), BF16, VMEM),
+            ((4, held, PAD_FF), BF16, VMEM),
             ((4, toks, width), BF16, HBM),
         ],
         [
@@ -1453,35 +1573,38 @@
             VMEM((4, toks, width), BF16),
             VMEM((toks, width), BF16),
         ]
-        + plane_scratch(PAD_FF),
-        150,
+        + plane_scratch(PAD_FF)
+        + plane_scratch(PAD_FF)[:2],
+        200,
         30 * 10**9,
     )
-    late_back, early_back, gate_back, last, layer, gain_sums = call(
+    late_back, early_back, gate_back, up_back, last, layer, gain_sums = call(
         back_kernel,
         2,
         [
             (middle_low, HBM),
             (raw_all, HBM),
-            (att, VMEM),
-            (qs, VMEM),
-            (ks, VMEM),
-            (values, VMEM),
-            (attended, VMEM),
-            (shares, VMEM),
-            (inverses, VMEM),
-            (raw, VMEM),
-            (grad_middle, VMEM),
-            (middle, VMEM),
-            (gains, VMEM),
-            (grad_gain2, VMEM),
+            (att, LOAD),
+            (qs, LOAD),
+            (ks, LOAD),
+            (values, LOAD),
+            (attended, LOAD),
+            (shares, LOAD),
+            (inverses, LOAD),
+            (raw, LOAD),
+            (grad_middle, LOAD),
+            (middle, LOAD),
+            (gains, LOAD),
+            (grad_gain2, LOAD),
             (grads, HBM),
             (layer_parts, HBM),
-            (gate_sum, VMEM),
+            (gate_sum, LOAD),
+            (up_mid, LOAD),
         ],
         [
             ((8, depth, LATE_W), BF16, HBM),
             ((8, depth, EARLY_W), BF16, HBM),
+            ((8, depth, PAD_FF), BF16, HBM),
             ((8, depth, PAD_FF), BF16, HBM),
             ((toks, width), BF16, HBM),
             ((toks, width), BF16, HBM),
@@ -1507,6 +1630,9 @@
         + plane_scratch(EARLY_W)
         + plane_scratch(LATE_W)
         + [
+            VMEM((1, held, PAD_FF), BF16),
+            VMEM((3, held, PAD_FF), BF16),
+            VMEM((held, PAD_FF), BF16),
             VMEM((held, EARLY_W), BF16),
             VMEM((held, LATE_W), BF16),
             VMEM((toks, width), BF16),
@@ -1522,7 +1648,7 @@
     grads_out = call(
         unpack_kernel,
         None,
-        [(array, VMEM) for array in (late_back, early_back, gate_back, layer, last, lane_order(True))],
+        [(array, VMEM) for array in (late_back, early_back, gate_back, up_back, layer, last, lane_order(True))],
         [
             ((depth, query_weight.shape[1]), F32, VMEM),
             ((depth, key_weight.shape[1]), F32, VMEM),

time: 281 us -> 269 us (0.957)
  Pallas kernels: 269 us -> 258 us
    pallas_call x4, Pallas kernels: 269 us -> 258 us  [call(): pl.pallas_call(kernel, out_shape=[jax.ShapeDtypeStruct(shape, dtype) for...]
where the time goes in v1:
time: 269 us; the launch traced here: 264 us
  Pallas kernels  258 us (96%)
    pallas_call x4, Pallas kernels, call(): pl.pallas_call(kernel, out_shape=[jax.ShapeDtypeStruct(shape, dtype) for...  258 us

profile of v1, /device:TPU:1, one launch (start us, length us, event | category | flops | bytes accessed | tf_op | source)
XLA Modules:
  0.0 264.1 jit_solution(11656856442638108219)
XLA Ops:
  0.6 0.7 pad_maximum_fusion
  1.3 0.7 copy.28.gain_pair
  2.7 1.3 fusion
  4.6 105.6 %forward_kernel.1 = (bf16[2048,640]{1,0:T(8,128)(2,1)}, bf16[2048,2304]{1,0:T(8,128)(2,1)}, bf16[1024,2048]{1,0:T(8,128)(2,1)}, bf16[1024,2048]{1,0:T(8,128)(2,1...) custom-call(bf16[128,2048]{1,0:T(8,128)(2,1)} %bitcast.14, ...), custom_call_target="tpu_custom_call" | custom-call | flops 4000000000 | bytes 67108864 | tf_op jit(solution)/shard_map/forward_kernel/pallas_call | solution.py:1412
  110.2 73.5 %mlp_kernel.1 = (f32[128,2048]{1,0:T(8,128)}, f32[8,2048]{1,0:T(8,128)}, bf16[1024,2048]{1,0:T(8,128)(2,1)}, bf16[2048,768]{1,0:T(8,128)(2,1)}, bf16[128,768]{1,...) custom-call(bf16[1024,2048]{1,0:T(8,128)(2,1)} %get-tuple-element.49.refs_0_, ...), custom_call_target="tpu_custom_call" | custom-call | flops 30000001024 | bytes 67108864 | tf_op jit(solution)/shard_map/mlp_kernel/pallas_call | solution.py:1412
  183.7 75.2 %back_kernel.1 = (bf16[8,16,384]{2,1,0:T(8,128)(2,1)}, bf16[8,16,1024]{2,1,0:T(8,128)(2,1)}, bf16[8,16,768]{2,1,0:T(8,128)(2,1)}, bf16[8,16,768]{2,1,0:T(8,128)(...) custom-call(bf16[1024,2048]{1,0:T(8,128)(2,1)} %get-tuple-element.55.refs_0_, ...), custom_call_target="tpu_custom_call" | custom-call | flops 8000000000 | bytes 67108864 | tf_op jit(solution)/shard_map/back_kernel/pallas_call | solution.py:1412
  258.9 3.5 %unpack_kernel.1 = (f32[16,256]{1,0:T(8,128)}, f32[16,256]{1,0:T(8,128)}, f32[16,2048]{1,0:T(8,128)}, f32[16,2048]{1,0:T(8,128)}, f32[16,5504]{1,0:T(8,128)}, /*...) custom-call(bf16[8,16,384]{2,1,0:T(8,128)(2,1)} %get-tuple-element.71.late, ...), custom_call_target="tpu_custom_call" | custom-call | bytes 67108864 | tf_op jit(solution)/shard_map/unpack_kernel/pallas_call | solution.py:1412
  262.4 0.8 constant_dynamic-slice_fusion
  263.1 0.5 slice_bitcast_fusion
